TPU v7x, 32 devices: a whole 2x2x4 slice. The times are simulated.
32 devices in a mesh: rep: 4 (over y, x), fsdp: 8 (over z, core).
Axes of the slice: x: 2, y: 2, z: 4, core: 2. Of those that a mesh axis runs over, the one named last changes fastest.
Arguments:
- acts: bfloat16 [1024, 4096], P(('rep', 'fsdp')), may hold values from -6 to 6
- grad_out: bfloat16 [1024, 14336], P(('rep', 'fsdp')), may hold values from -0.375 to 0.375
- momentum: bfloat16 [4, 4096, 14336], P('rep', 'fsdp'), may hold values from -6 to 6
- band: int32 [32], replicated, may hold values from 0 to 975, as said below
Outputs:
- new_momentum: bfloat16 [4, 4096, 14336], P('rep', 'fsdp')
- update: bfloat16 [4096, 14336], P('fsdp')
Inputs may be any that keep to these rules, and one draw needn't show every extreme that they name: `band`: 32 distinct positions u * 64 + v with u and v below 16; 0 and 975 are always among them.
All inputs are finite; a program needn't handle non-finite values.
Results may differ from a plain program's by a relative error of at most 0.007.
Values may be sent and summed in bfloat16 or wider, within the bound.
A program may use at most 384 MiB of HBM per device.

v0:
```python
import jax
import jax.numpy as jnp
from jax import lax
from jax.sharding import PartitionSpec as P

BLOCK = 64


momentum_decay = 0.999


def band_basis(band):
    freq = jnp.arange(BLOCK, dtype=jnp.float32)[:, None]
    place = jnp.arange(BLOCK, dtype=jnp.float32)[None, :]
    factor = jnp.where(freq == 0.0, jnp.sqrt(1.0 / BLOCK), jnp.sqrt(2.0 / BLOCK))
    table = factor * jnp.cos(jnp.pi * (2.0 * place + 1.0) * freq / (2.0 * BLOCK))
    levels = jnp.arange(BLOCK, dtype=jnp.int32)[None, :]
    pick_u = (band[:, None] // BLOCK == levels).astype(jnp.float32)
    pick_v = (band[:, None] % BLOCK == levels).astype(jnp.float32)
    rows_u = jnp.dot(pick_u, table, precision=lax.Precision.HIGHEST)
    rows_v = jnp.dot(pick_v, table, precision=lax.Precision.HIGHEST)
    return (rows_u[:, :, None] * rows_v[:, None, :]).astype(jnp.bfloat16)


def shards(acts, grad_out, momentum, band):
    columns = lax.all_to_all(acts, "fsdp", split_axis=1, concat_axis=0, tiled=True)
    rows = momentum.shape[1]
    width = momentum.shape[2]
    grad = lax.dot_general(
        columns,
        lax.all_gather(grad_out, "fsdp", axis=0, tiled=True),
        (((0,), (0,)), ((), ())),
        preferred_element_type=jnp.float32,
    )
    full = momentum_decay * momentum[0].astype(jnp.float32) + grad
    blocks = full.astype(jnp.bfloat16).reshape(rows // BLOCK, BLOCK, width // BLOCK, BLOCK)
    basis = band_basis(band)
    own = jnp.einsum("iajb,kab->ijk", blocks, basis, preferred_element_type=jnp.float32)
    shaped = jnp.einsum(
        "ijk,kab->iajb", own.astype(jnp.bfloat16), basis, preferred_element_type=jnp.float32
    )
    fresh = (full - shaped.reshape(rows, width)).astype(jnp.bfloat16)[None]
    replicas = lax.axis_size("rep")
    total = lax.psum(own, "rep")
    mean_coeff = (total / replicas).astype(jnp.bfloat16)
    update = (
        jnp.einsum("ijk,kab->iajb", mean_coeff, basis, preferred_element_type=jnp.float32)
        .reshape(rows, width)
        .astype(jnp.bfloat16)
    )
    return (fresh, update)


def solution(mesh):
    placed = (P(("rep", "fsdp"), None), P(("rep", "fsdp"), None), P("rep", "fsdp", None), P())
    return jax.shard_map(
        shards,
        mesh=mesh,
        in_specs=placed,
        out_specs=(P("rep", "fsdp", None), P("fsdp", None)),
        check_vma=False,
    )
```

profile of v0, /device:TPU:0, one launch (start us, length us, event | category | flops | bytes accessed | tf_op | source)
XLA Modules:
  0.0 367.8 jit_solution(6099782386802087548)
XLA Ops:
  7.2 0.0 all-gather.2.cloned.1.call-start
  7.2 0.7 all-gather.2.cloned.1.call-update
  7.9 1.7 copy.29
  9.6 6.3 %all-to-all-start = ((bf16[32,8,512]{2,0,1:T(8,128)(2,1)}), bf16[32,8,512]{2,0,1:T(8,128)(2,1)S(1)}, u32[]{:S(2)}, u32[]{:S(2)}) async-start(bf16[32,8,512]{2,0,1:T(8,128)(2,1)} %bitcast.38), calls=%async_computation | async-start | bytes 524288 | tf_op jit(solution)/shard_map/all_to_all | solution.py:26
  15.9 0.7 and_select_fusion.1
  16.6 0.3 fusion.17
  16.8 0.4 fusion.18
  17.2 11.7 %all-to-all-done = bf16[32,8,512]{2,0,1:T(8,128)(2,1)S(1)} async-done(((bf16[32,8,512]{2,0,1:T(8,128)(2,1)}), bf16[32,8,512]{2,0,1:T(8,128)(2,1)S(1)}, u32[]{:S(2)}, u32[]{:S(2)}) %all-to-all-start) | async-done | bytes 262176 | tf_op jit(solution)/shard_map/all_to_all | solution.py:26
  28.9 57.9 %all-gather.2.cloned.1.call-done = bf16[256,14336]{1,0:T(8,128)(2,1)} async-done(((bf16[32,14336]{1,0:T(8,128)(2,1)}), bf16[256,14336]{1,0:T(8,128)(2,1)}) %all-gather.2.cloned.1.call-update) | async-done | bytes 7340048 | tf_op jit(solution)/shard_map/all_gather | solution.py:31
  86.8 22.4 %fusion.30 = (bf16[512,14336]{1,0:T(8,128)(2,1)}, f32[512,14336]{1,0:T(8,128)}) fusion(bf16[256,512]{1,0:T(8,128)(2,1)S(1)} %bitcast.39, bf16[256,14336]{1,0:T(8,128)(2,1)} %all-gather.2.cloned.1.call-done, bf16[1,512,14336]{2,1,0:T(8,128)(2,1)} %param.6), kind=kOutput, calls=%fused_computation.44 | convolution fusion | flops 3787456512 | bytes 66322432 | tf_op jit(solution)/shard_map/dot_general | solution.py:29
  109.1 37.3 %reshape.62 = bf16[8,64,224,64]{3,2,1,0:T(8,128)(2,1)} reshape(bf16[512,14336]{1,0:T(8,128)(2,1)} %get-tuple-element.4) | data formatting | bytes 29360128 | tf_op jit(solution)/shard_map/reshape | solution.py:36
  146.4 14.0 %convolution_bitcast_fusion.1 = f32[8,224,32]{1,2,0:T(8,128)S(1)} fusion(bf16[8,64,224,64]{3,2,1,0:T(8,128)(2,1)} %reshape.62, f32[32,64]{1,0:T(8,128)S(1)} %fusion.17, f32[32,64]{0,1:T(8,128)S(1)} %fusion.18), kind=kOutput, calls=%fused_computation.5 | convolution fusion | flops 470024192 | bytes 14925824 | tf_op jit(solution)/shard_map/iajb,kab->ijk/dot_general | solution.py:38
  160.3 0.0 copy-start
  160.4 13.4 %convolution_bitcast_fusion = f32[8,64,224,64]{2,3,0,1:T(8,128)} fusion(f32[32,64]{1,0:T(8,128)S(1)} %fusion.17, f32[32,64]{0,1:T(8,128)S(1)} %fusion.18, f32[8,224,32]{1,2,0:T(8,128)S(1)} %convolution_bitcast_fusion.1), kind=kOutput, calls=%fused_computation.4 | convolution fusion | flops 470081536 | bytes 29605888 | tf_op jit(solution)/shard_map/ijk,kab->iajb/dot_general | solution.py:39
  173.8 0.0 copy-done
  173.8 0.0 all-reduce.2.cloned.1.call-start
  173.8 43.2 %copy.21 = f32[8,64,224,64]{3,2,1,0:T(8,128)} copy(f32[8,64,224,64]{2,3,0,1:T(8,128)} %convolution_bitcast_fusion) | data formatting | bytes 58720256 | tf_op jit(solution)/shard_map/ijk,kab->iajb/transpose | solution.py:39
  217.0 0.0 all-reduce.2.cloned.1.call-update
  217.1 45.0 %reshape.63 = f32[512,14336]{1,0:T(8,128)} reshape(f32[8,64,224,64]{3,2,1,0:T(8,128)} %copy.21) | data formatting | bytes 58720256 | tf_op jit(solution)/shard_map/reshape | solution.py:42
  262.1 24.4 %fusion = bf16[1,512,14336]{2,1,0:T(8,128)(2,1)} fusion(f32[512,14336]{1,0:T(8,128)} %get-tuple-element.5, f32[512,14336]{1,0:T(8,128)} %reshape.63), kind=kLoop, calls=%fused_computation.3 | loop fusion | flops 14680064 | bytes 73400320 | tf_op jit(solution)/shard_map/broadcast_in_dim | solution.py:42
  286.5 0.0 all-reduce.2.cloned.1.call-done
  286.5 9.6 %convert_bitcast_fusion = bf16[8,64,224,64]{2,3,0,1:T(8,128)(2,1)} fusion(f32[32,64]{1,0:T(8,128)S(1)} %fusion.17, f32[32,64]{0,1:T(8,128)S(1)} %fusion.18, f32[8,224,32]{1,2,0:T(8,128)} %all-reduce.2.cloned.1.call-done), kind=kOutput, calls=%fused_computation.2 | convolution fusion | flops 477478912 | bytes 14925824 | tf_op jit(solution)/shard_map/ijk,kab->iajb/dot_general | solution.py:47
  296.0 29.2 %copy.22 = bf16[8,64,224,64]{3,2,1,0:T(8,128)(2,1)} copy(bf16[8,64,224,64]{2,3,0,1:T(8,128)(2,1)} %convert_bitcast_fusion) | data formatting | bytes 29360128 | tf_op jit(solution)/shard_map/convert_element_type | solution.py:49
  325.2 35.7 %convert_element_type.38 = bf16[512,14336]{1,0:T(8,128)(2,1)} reshape(bf16[8,64,224,64]{3,2,1,0:T(8,128)(2,1)} %copy.22) | data formatting | bytes 29360128 | tf_op jit(solution)/shard_map/convert_element_type | solution.py:49
  (1 shorter events, 0.0 us)
Async XLA Ops:
  7.2 79.6 %all-gather.2.cloned.1.call-start = ((), (), s32[]{:S(2)}) async-start(), calls=%async_computation.1 | async-start | bytes 8257536 | tf_op jit(solution)/shard_map/all_gather | solution.py:31
  9.6 19.3 %all-to-all-start = ((bf16[32,8,512]{2,0,1:T(8,128)(2,1)}), bf16[32,8,512]{2,0,1:T(8,128)(2,1)S(1)}, u32[]{:S(2)}, u32[]{:S(2)}) async-start(bf16[32,8,512]{2,0,1:T(8,128)(2,1)} %bitcast.38), calls=%async_computation | async-start | bytes 524288 | tf_op jit(solution)/shard_map/all_to_all | solution.py:26
  160.3 13.5 %copy-start = (f32[8,224,32]{1,2,0:T(8,128)}, f32[8,224,32]{1,2,0:T(8,128)S(1)}, u32[]{:S(2)}) copy-start(f32[8,224,32]{1,2,0:T(8,128)S(1)} %convolution_bitcast_fusion.1) | copy-start | bytes 688132
  173.8 112.7 %all-reduce.2.cloned.1.call-start = ((), (), s32[]{:S(2)}) async-start(), calls=%async_computation.2 | async-start | bytes 524288 | tf_op jit(solution)/shard_map/psum | solution.py:44
Sparse Core Ops, SparseCore 0:
  9.6 77.0 all-gather.1
  217.2 41.8 all-reduce.1
where the time goes:
time: 372 us; the launch traced here: 368 us
  local copies, waits for them, and re-layouts  192 us (52%)
  waiting for transfers between devices  70.3 us (19%)
  matrix products  59.9 us (16%)
  other arithmetic  25.1 us (7%)
  between operations  14.1 us (4%)
  starting transfers between devices  6.37 us (2%)
    convert_element_type x2, local copies, waits for them, and re-layouts, shards(): update = jnp.einsum('ijk,kab->iajb', mean_coeff, basis, preferred_element...  64.9 us
    all_gather x1, waiting for transfers between devices, shards(): lax.all_gather(grad_out, 'fsdp', axis=0, tiled=True)  57.9 us
    reshape x1, local copies, waits for them, and re-layouts, shards(): fresh = (full - shaped.reshape(rows, width)).astype(jnp.bfloat16)[None]  45 us
    transpose x1, local copies, waits for them, and re-layouts, shards(): jnp.einsum('ijk,kab->iajb', own.astype(jnp.bfloat16), basis, preferred_el...  43.2 us
    reshape x1, local copies, waits for them, and re-layouts, shards(): full.astype(jnp.bfloat16)  37.3 us
    broadcast_in_dim x1, other arithmetic, shards(): fresh = (full - shaped.reshape(rows, width)).astype(jnp.bfloat16)[None]  24.4 us
    dot_general x1, matrix products, shards(): lax.dot_general(columns, lax.all_gather(grad_out, 'fsdp', axis=0, tiled=T...  22.4 us
    dot_general x1, matrix products, shards(): jnp.einsum('iajb,kab->ijk', blocks, basis, preferred_element_type=jnp.flo...  14 us
  transfers between devices with their start and end apart: 3, of which 2 were waited for; matrix products, arithmetic and copies ran while one was open for 20% of the time, Pallas kernels for 0%

commit v1 on v0

v1 whole, which is shorter than its diff:
```python
import functools

import jax
import jax.numpy as jnp
import ml_dtypes
import numpy as np
from jax import lax
from jax.experimental import pallas as pl
from jax.experimental.pallas import tpu as pltpu
from jax.sharding import PartitionSpec as P

BLOCK = 64
LOW = 16
GROUP = 512
LAG = 1

momentum_decay = 0.999
MESH = pl.DeviceIdType.MESH
BF16 = jnp.bfloat16


def dct_low():
    u = np.arange(LOW, dtype=np.float64)[:, None]
    a = np.arange(BLOCK, dtype=np.float64)[None, :]
    scale = np.where(u == 0, np.sqrt(1.0 / BLOCK), np.sqrt(2.0 / BLOCK))
    return scale * np.cos(np.pi * (2 * a + 1) * u / (2 * BLOCK))


def tables(rows):
    low_dct = dct_low()
    all_cols = np.kron(np.eye(GROUP // BLOCK), low_dct)
    all_rows = np.kron(np.eye(rows // BLOCK), low_dct)
    ch, cl = np_split(all_cols)
    rh, rl = np_split(all_rows)
    fold = np.concatenate([ch.T, cl.T], axis=1)
    unfold = np.concatenate([ch, cl], axis=0)
    spread = np.concatenate([rh.T, rl.T], axis=1)
    return fold, unfold, rh, rl, spread


def np_split(table):
    high = table.astype(ml_dtypes.bfloat16)
    low = (table - high.astype(np.float64)).astype(ml_dtypes.bfloat16)
    return high, low


def dot(a, b):
    return jnp.dot(a, b, preferred_element_type=jnp.float32)


def gather_kernel(
    n_rep, n_fsdp, width, chunks,
    band, acts, gout, momentum, fold, rh, rl,
    at_out, g_out, own_out, mean_out,
    acts_all, g_all, at_v, mom, c_all, mask,
    a_recv, a_send, a_local, g_local, g_recv, line_send, left_send, sib_send,
    m_sem, c_recv, c_send, o_sem, t_sem,
):
    rep = lax.axis_index("rep")
    me = lax.axis_index("fsdp")
    core = lax.rem(me, 2)
    pos = me // 2
    places = n_fsdp // 2
    sib = me + 1 - 2 * core
    rows = at_v.shape[0]
    toks = gout.shape[0]
    low_width = width // BLOCK * LOW

    barrier = pltpu.get_barrier_semaphore()
    for d in range(1, n_fsdp):
        pl.semaphore_signal(
            barrier, inc=1, device_id=(rep, lax.rem(me + d, n_fsdp)), device_id_type=MESH
        )
    for d in range(1, n_rep):
        pl.semaphore_signal(
            barrier, inc=1, device_id=(lax.rem(rep + d, n_rep), me), device_id_type=MESH
        )

    def cols(n):
        return pl.ds(pl.multiple_of(n * width, width), width)

    def low_cols(n):
        return pl.ds(pl.multiple_of(n * low_width, low_width), low_width)

    def load_mom(n):
        return pltpu.make_async_copy(
            momentum.at[0, :, cols(n)], mom.at[lax.rem(n, 2)], m_sem.at[lax.rem(n, 2)]
        )

    own_acts = pltpu.make_async_copy(
        acts.at[:, pl.ds(pl.multiple_of(me * rows, rows), rows)], acts_all.at[me], a_local
    )
    own_acts.start()
    own_g = pltpu.make_async_copy(gout, g_all.at[me], g_local)
    own_g.start()
    load_mom(0).start()

    pl.semaphore_wait(barrier, n_fsdp - 1 + n_rep - 1)

    def acts_copy(d):
        peer = lax.rem(me + d, n_fsdp)
        return pltpu.make_async_remote_copy(
            src_ref=acts.at[:, pl.ds(pl.multiple_of(peer * rows, rows), rows)],
            dst_ref=acts_all.at[me],
            send_sem=a_send.at[d],
            recv_sem=a_recv.at[me],
            device_id=(rep, peer),
            device_id_type=MESH,
        )

    def g_copy(src, b, n, send, target):
        return pltpu.make_async_remote_copy(
            src_ref=src,
            dst_ref=g_all.at[b, :, cols(n)],
            send_sem=send,
            recv_sem=g_recv.at[b, n],
            device_id=(rep, target),
            device_id_type=MESH,
        )

    def slot(b, n):
        return g_all.at[b, :, cols(n)]

    def own_right(n):
        return g_copy(gout.at[:, cols(n)], me, n, line_send.at[pos, n], me + 2)

    def own_left(n):
        return g_copy(gout.at[:, cols(n)], me, n, left_send.at[n], me - 2)

    def own_sib(n):
        return g_copy(gout.at[:, cols(n)], me, n, sib_send.at[pos, n], sib)

    def forward(q, n, target):
        b = 2 * q + core
        return g_copy(slot(b, n), b, n, line_send.at[q, n], target)

    def to_sib(q, n):
        b = 2 * q + core
        return g_copy(slot(b, n), b, n, sib_send.at[q, n], sib)

    def wait_block(b, n):
        pltpu.make_async_copy(slot(b, n), slot(b, n), g_recv.at[b, n]).wait()

    def send_own(n):
        @pl.when(pos + 1 < places)
        def _():
            own_right(n).start()

        @pl.when(pos > 0)
        def _():
            own_left(n).start()

        own_sib(n).start()

    def c_copy(d, n):
        peer = lax.rem(rep + d, n_rep)
        return pltpu.make_async_remote_copy(
            src_ref=c_all.at[rep, :, low_cols(n)],
            dst_ref=c_all.at[rep, :, low_cols(n)],
            send_sem=c_send.at[d, n],
            recv_sem=c_recv.at[rep, n],
            device_id=(peer, me),
            device_id_type=MESH,
        )

    for d in range(1, n_fsdp):
        acts_copy(d).start()
    send_own(0)
    send_own(1)

    low_rows = lax.broadcasted_iota(jnp.int32, mask.shape, 0)
    low_lanes = lax.broadcasted_iota(jnp.int32, mask.shape, 1)
    place = lax.rem(low_rows, LOW) * BLOCK + lax.rem(low_lanes, LOW)
    kept = jnp.zeros(mask.shape, jnp.float32)
    for k in range(band.shape[0]):
        kept = jnp.where(place == band[k], 1.0, kept)
    mask[...] = kept

    own_acts.wait()
    own_g.wait()
    for d in range(1, n_fsdp):
        b = lax.rem(me + d, n_fsdp)
        pltpu.make_async_copy(acts_all.at[b], acts_all.at[b], a_recv.at[b]).wait()
    for b in range(n_fsdp):
        at_v[:, b * toks:(b + 1) * toks] = (
            acts_all[b].astype(jnp.float32).T.astype(BF16)
        )
    at_copy = pltpu.make_async_copy(at_v, at_out, t_sem)
    at_copy.start()

    def out_copy(n):
        return pltpu.make_async_copy(g_all.at[:, :, cols(n)], g_out.at[:, :, cols(n)], o_sem.at[n])

    def step(t, _):
        @pl.when(t + 2 < chunks)
        def _():
            send_own(t + 2)

        for h in range(1, places):
            n = t + 1 - h

            @pl.when((n >= 0) & (n < chunks) & (pos >= h))
            def _():
                q = pos - h
                wait_block(2 * q + core, n)

                @pl.when(pos + 1 < places)
                def _():
                    forward(q, n, me + 2).start()

                to_sib(q, n).start()

            @pl.when((n >= 0) & (n < chunks) & (pos + h < places))
            def _():
                q = pos + h
                wait_block(2 * q + core, n)

                @pl.when(pos > 0)
                def _():
                    forward(q, n, me - 2).start()

                to_sib(q, n).start()

        n = t - (places - 1)

        @pl.when((n >= 0) & (n < chunks))
        def _():
            @pl.when(n + 1 < chunks)
            def _():
                load_mom(n + 1).start()

            load_mom(n).wait()
            for q in range(places):
                wait_block(2 * q + 1 - core, n)
            out_copy(n).start()
            folded = []
            for s in range(width // GROUP):
                at_cols = pl.ds(pl.multiple_of(n * width + s * GROUP, GROUP), GROUP)
                tok = g_all[:, :, at_cols].reshape(n_fsdp * toks, GROUP)
                grad = dot(at_v[...], tok)
                state = mom[lax.rem(n, 2), :, s * GROUP:(s + 1) * GROUP]
                full = momentum_decay * state.astype(jnp.float32) + grad
                both = dot(full.astype(BF16), fold[...])
                half = both.shape[1] // 2
                folded.append(both[:, :half] + both[:, half:])
            part = jnp.concatenate(folded, axis=1)
            high = part.astype(BF16)
            low = (part - high.astype(jnp.float32)).astype(BF16)
            coeff = dot(rh[...], high) + dot(rh[...], low) + dot(rl[...], high)
            c_all[rep, :, low_cols(n)] = (coeff * mask[...]).astype(BF16)
            for d in range(1, n_rep):
                c_copy(d, n).start()

        m = n - LAG

        @pl.when((m >= 0) & (m < chunks))
        def _():
            for d in range(1, n_rep):
                r = lax.rem(rep + d, n_rep)
                piece = c_all.at[r, :, low_cols(m)]
                pltpu.make_async_copy(piece, piece, c_recv.at[r, m]).wait()
            total = c_all[0, :, low_cols(m)].astype(jnp.float32)
            for r in range(1, n_rep):
                total += c_all[r, :, low_cols(m)].astype(jnp.float32)
            mean_out[:, low_cols(m)] = (total * (1.0 / n_rep)).astype(BF16)
            own_out[:, low_cols(m)] = c_all[rep, :, low_cols(m)]

        return 0

    lax.fori_loop(0, chunks + places - 1 + LAG, step, 0)

    at_copy.wait()
    for d in range(1, n_fsdp):
        acts_copy(d).wait_send()

    def drain(n, _):
        out_copy(n).wait()

        @pl.when(pos + 1 < places)
        def _():
            own_right(n).wait_send()

        @pl.when(pos > 0)
        def _():
            own_left(n).wait_send()

        own_sib(n).wait_send()
        for h in range(1, places):
            @pl.when(pos >= h)
            def _():
                @pl.when(pos + 1 < places)
                def _():
                    forward(pos - h, n, me + 2).wait_send()

                to_sib(pos - h, n).wait_send()

            @pl.when(pos + h < places)
            def _():
                @pl.when(pos > 0)
                def _():
                    forward(pos + h, n, me - 2).wait_send()

                to_sib(pos + h, n).wait_send()

        for d in range(1, n_rep):
            c_copy(d, n).wait_send()
        return 0

    lax.fori_loop(0, chunks, drain, 0)


def finish_kernel(at, g, momentum, own, mean, unfold, spread, fresh, update):
    width = momentum.shape[2]
    low = GROUP // BLOCK * LOW

    def spread_rows(c):
        return dot(spread[...], jnp.concatenate([c, c], axis=0)).astype(BF16)

    own_rows = spread_rows(own[...])
    mean_rows = spread_rows(mean[...])
    for s in range(width // GROUP):
        here = slice(s * GROUP, (s + 1) * GROUP)
        lanes = slice(s * low, (s + 1) * low)
        tok = g[:, :, here].reshape(at.shape[1], GROUP)
        full = momentum_decay * momentum[0, :, here].astype(jnp.float32) + dot(at[...], tok)
        piece = own_rows[:, lanes]
        shaped = dot(jnp.concatenate([piece, piece], axis=1), unfold[...])
        fresh[0, :, here] = (full - shaped).astype(BF16)
        piece = mean_rows[:, lanes]
        update[:, here] = dot(jnp.concatenate([piece, piece], axis=1), unfold[...]).astype(BF16)


def shards(n_rep, n_fsdp, acts, grad_out, momentum, band):
    toks, cols = grad_out.shape
    rows = momentum.shape[1]
    width = 1024 if cols % 1024 == 0 else GROUP
    if n_fsdp > 8:
        width = 2048
    chunks = cols // width
    places = n_fsdp // 2
    fold, unfold, rh, rl, spread = [jnp.asarray(t) for t in tables(rows)]
    low_rows = rows // BLOCK * LOW
    low_cols = cols // BLOCK * LOW
    low_width = width // BLOCK * LOW
    tokens = toks * n_fsdp
    vmem = pl.BlockSpec(memory_space=pltpu.VMEM)
    hbm = pl.BlockSpec(memory_space=pl.ANY)
    dma = pltpu.SemaphoreType.DMA
    at, g, own, mean = pl.pallas_call(
        functools.partial(gather_kernel, n_rep, n_fsdp, width, chunks),
        out_shape=(
            jax.ShapeDtypeStruct((rows, tokens), BF16),
            jax.ShapeDtypeStruct((n_fsdp, toks, cols), BF16),
            jax.ShapeDtypeStruct((low_rows, low_cols), BF16),
            jax.ShapeDtypeStruct((low_rows, low_cols), BF16),
        ),
        in_specs=[pl.BlockSpec(memory_space=pltpu.SMEM), hbm, hbm, hbm, vmem, vmem, vmem],
        out_specs=(hbm, hbm, vmem, vmem),
        scratch_shapes=[
            pltpu.VMEM((n_fsdp, toks, rows), BF16),
            pltpu.VMEM((n_fsdp, toks, cols), BF16),
            pltpu.VMEM((rows, tokens), BF16),
            pltpu.VMEM((2, rows, width), BF16),
            pltpu.VMEM((n_rep, low_rows, low_cols), BF16),
            pltpu.VMEM((low_rows, low_width), jnp.float32),
            dma((n_fsdp,)), dma((n_fsdp,)), dma, dma,
            dma((n_fsdp, chunks)), dma((places, chunks)), dma((chunks,)), dma((places, chunks)),
            dma((2,)), dma((n_rep, chunks)), dma((n_rep, chunks)), dma((chunks,)), dma,
        ],
        compiler_params=pltpu.CompilerParams(
            collective_id=0, has_side_effects=True, vmem_limit_bytes=56 * 2**20
        ),
        cost_estimate=pl.CostEstimate(
            flops=4 * rows * tokens * cols, bytes_accessed=2 * rows * cols, transcendentals=0
        ),
        name="gather",
    )(band, acts, grad_out, momentum, fold, rh, rl)
    fresh, update = pl.pallas_call(
        finish_kernel,
        grid=(cols // 1024,),
        out_shape=(
            jax.ShapeDtypeStruct((1, rows, cols), BF16),
            jax.ShapeDtypeStruct((rows, cols), BF16),
        ),
        in_specs=[
            vmem,
            pl.BlockSpec((n_fsdp, toks, 1024), lambda n: (0, 0, n)),
            pl.BlockSpec((1, rows, 1024), lambda n: (0, 0, n)),
            pl.BlockSpec((low_rows, 256), lambda n: (0, n)),
            pl.BlockSpec((low_rows, 256), lambda n: (0, n)),
            vmem,
            vmem,
        ],
        out_specs=(
            pl.BlockSpec((1, rows, 1024), lambda n: (0, 0, n)),
            pl.BlockSpec((rows, 1024), lambda n: (0, n)),
        ),
        compiler_params=pltpu.CompilerParams(vmem_limit_bytes=56 * 2**20),
        cost_estimate=pl.CostEstimate(
            flops=8 * rows * tokens * cols, bytes_accessed=7 * rows * cols, transcendentals=0
        ),
        name="finish",
    )(at, g, momentum, own, mean, unfold, spread)
    return fresh, update


def solution(mesh):
    placed = (P(("rep", "fsdp"), None), P(("rep", "fsdp"), None), P("rep", "fsdp", None), P())
    return jax.shard_map(
        functools.partial(shards, mesh.shape["rep"], mesh.shape["fsdp"]),
        mesh=mesh,
        in_specs=placed,
        out_specs=(P("rep", "fsdp", None), P("fsdp", None)),
        check_vma=False,
    )
```

time: 372 us -> 116 us (0.31); the launches traced: 368 us -> 116 us
  local copies, waits for them, and re-layouts: 192 us -> 0 us
  Pallas kernels: 0 us -> 115 us
  waiting for transfers between devices: 70.3 us -> 0 us
  matrix products: 59.9 us -> 0 us
  other arithmetic: 25.1 us -> 0 us
  between operations: 14.1 us -> 0.64 us
  starting transfers between devices: 6.37 us -> 0 us
    pallas_call x0 -> x2, Pallas kernels: none -> 115 us  [the longest x1 89.8 us: shards(): pl.pallas_call(functools.partial(gather_kernel, n_rep, n_fsdp, width, chu...]
    reshape x2 -> x0, local copies, waits for them, and re-layouts: 82.3 us -> none  [the longest x1 45 us: shards(): fresh = (full - shaped.reshape(rows, width)).astype(jnp.bfloat16)[None]]
    convert_element_type x2 -> x0, local copies, waits for them, and re-layouts: 64.9 us -> none  [shards(): update = jnp.einsum('ijk,kab->iajb', mean_coeff, basis, preferred_element...]
    dot_general x6 -> x0, matrix products: 59.9 us -> none  [the longest x1 22.4 us: shards(): lax.dot_general(columns, lax.all_gather(grad_out, 'fsdp', axis=0, tiled=T...]
    all_gather x1 -> x0, waiting for transfers between devices: 57.9 us -> none  [shards(): lax.all_gather(grad_out, 'fsdp', axis=0, tiled=True)]
    transpose x1 -> x0, local copies, waits for them, and re-layouts: 43.2 us -> none  [shards(): jnp.einsum('ijk,kab->iajb', own.astype(jnp.bfloat16), basis, preferred_el...]
    broadcast_in_dim x1 -> x0, other arithmetic: 24.4 us -> none  [shards(): fresh = (full - shaped.reshape(rows, width)).astype(jnp.bfloat16)[None]]
    all_to_all x1 -> x0, waiting for transfers between devices: 11.7 us -> none  [shards(): lax.all_to_all(acts, 'fsdp', split_axis=1, concat_axis=0, tiled=True)]
  transfers between devices with their start and end apart: 3 -> 0, of which waited for: 2 -> 0; matrix products, arithmetic and copies ran while one was open for 20% -> 0% of each run, Pallas kernels for 0% -> 0%
where the time goes in v1:
time: 116 us
  Pallas kernels  115 us (99%)
    pallas_call x1, Pallas kernels, shards(): pl.pallas_call(functools.partial(gather_kernel, n_rep, n_fsdp, width, chu...  89.8 us
    pallas_call x1, Pallas kernels, shards(): pl.pallas_call(finish_kernel, grid=(cols // 1024,), out_shape=(jax.ShapeD...  25.2 us

profile of v1, /device:TPU:0, one launch (start us, length us, event | category | flops | bytes accessed | tf_op | source)
XLA Modules:
  0.0 115.6 jit_solution(11000621757170343088)
XLA Ops:
  0.6 89.8 %gather.1 = (bf16[512,256]{1,0:T(8,128)(2,1)}, bf16[8,32,14336]{2,1,0:T(8,128)(2,1)}, bf16[128,3584]{1,0:T(8,128)(2,1)}, bf16[128,3584]{1,0:T(8,128)(2,1)}) custom-call(s32[32]{0:T(128)} %band.1, bf16[32,4096]{1,0:T(8,128)(2,1)} %acts.1, bf16[32,14336]{1,0:T(8,128)(2,1)} %gout.1, bf16[1,512,14336]{2,1,0:T(8,128)(2,1)} %momentum.3, ...), custom_call_target="tpu_custom_call" | custom-call | flops 7516192768 | bytes 14680064 | tf_op jit(solution)/shard_map/gather/pallas_call | solution.py:349
  90.4 25.2 %finish.1 = (bf16[1,512,14336]{2,1,0:T(8,128)(2,1)}, bf16[512,14336]{1,0:T(8,128)(2,1)}) custom-call(bf16[512,256]{1,0:T(8,128)(2,1)} %get-tuple-element.6.at, bf16[8,32,14336]{2,1,0:T(8,128)(2,1)} %get-tuple-element.7.g, bf16[1,512,14336]{2,1,0:T(8,128)(2,1)} %momentum.3, bf16[128,3584]{1,0:T(8,128)(2,1)} %get-tuple-element.8.own, ...), custom_call_target="tpu_custom_call" | custom-call | flops 15032385536 | bytes 51380224 | tf_op jit(solution)/shard_map/finish/pallas_call | solution.py:378

commit v2 on v1

--- a/solution.py
+++ b/solution.py
@@ -50,11 +50,11 @@
 
 def gather_kernel(
     n_rep, n_fsdp, width, chunks,
-    band, acts, gout, momentum, fold, rh, rl,
-    at_out, g_out, own_out, mean_out,
-    acts_all, g_all, at_v, mom, c_all, mask,
+    band, acts, gout, momentum, fold, rh, rl, unfold, spread,
+    fresh_out, mean_out,
+    acts_all, g_all, at_v, mom, full_v, c_all, mask,
     a_recv, a_send, a_local, g_local, g_recv, line_send, left_send, sib_send,
-    m_sem, c_recv, c_send, o_sem, t_sem,
+    m_sem, c_recv, c_send,
 ):
     rep = lax.axis_index("rep")
     me = lax.axis_index("fsdp")
@@ -185,11 +185,6 @@
         at_v[:, b * toks:(b + 1) * toks] = (
             acts_all[b].astype(jnp.float32).T.astype(BF16)
         )
-    at_copy = pltpu.make_async_copy(at_v, at_out, t_sem)
-    at_copy.start()
-
-    def out_copy(n):
-        return pltpu.make_async_copy(g_all.at[:, :, cols(n)], g_out.at[:, :, cols(n)], o_sem.at[n])
 
     def step(t, _):
         @pl.when(t + 2 < chunks)
@@ -232,7 +227,6 @@
             load_mom(n).wait()
             for q in range(places):
                 wait_block(2 * q + 1 - core, n)
-            out_copy(n).start()
             folded = []
             for s in range(width // GROUP):
                 at_cols = pl.ds(pl.multiple_of(n * width + s * GROUP, GROUP), GROUP)
@@ -240,6 +234,7 @@
                 grad = dot(at_v[...], tok)
                 state = mom[lax.rem(n, 2), :, s * GROUP:(s + 1) * GROUP]
                 full = momentum_decay * state.astype(jnp.float32) + grad
+                full_v[:, s * GROUP:(s + 1) * GROUP] = full
                 both = dot(full.astype(BF16), fold[...])
                 half = both.shape[1] // 2
                 folded.append(both[:, :half] + both[:, half:])
@@ -247,9 +242,19 @@
             high = part.astype(BF16)
             low = (part - high.astype(jnp.float32)).astype(BF16)
             coeff = dot(rh[...], high) + dot(rh[...], low) + dot(rl[...], high)
-            c_all[rep, :, low_cols(n)] = (coeff * mask[...]).astype(BF16)
+            own = (coeff * mask[...]).astype(BF16)
+            c_all[rep, :, low_cols(n)] = own
             for d in range(1, n_rep):
                 c_copy(d, n).start()
+
+            own_rows = dot(spread[...], jnp.concatenate([own, own], axis=0)).astype(BF16)
+            low = GROUP // BLOCK * LOW
+            for s in range(width // GROUP):
+                here = slice(s * GROUP, (s + 1) * GROUP)
+                there = pl.ds(pl.multiple_of(n * width + s * GROUP, GROUP), GROUP)
+                piece = own_rows[:, s * low:(s + 1) * low]
+                shaped = dot(jnp.concatenate([piece, piece], axis=1), unfold[...])
+                fresh_out[:, there] = (full_v[:, here] - shaped).astype(BF16)
 
         m = n - LAG
 
@@ -263,19 +268,15 @@
             for r in range(1, n_rep):
                 total += c_all[r, :, low_cols(m)].astype(jnp.float32)
             mean_out[:, low_cols(m)] = (total * (1.0 / n_rep)).astype(BF16)
-            own_out[:, low_cols(m)] = c_all[rep, :, low_cols(m)]
 
         return 0
 
     lax.fori_loop(0, chunks + places - 1 + LAG, step, 0)
 
-    at_copy.wait()
     for d in range(1, n_fsdp):
         acts_copy(d).wait_send()
 
     def drain(n, _):
-        out_copy(n).wait()
-
         @pl.when(pos + 1 < places)
         def _():
             own_right(n).wait_send()
@@ -309,25 +310,28 @@
     lax.fori_loop(0, chunks, drain, 0)
 
 
-def finish_kernel(at, g, momentum, own, mean, unfold, spread, fresh, update):
-    width = momentum.shape[2]
+def finish_kernel(fresh_in, mean, unfold, spread, fresh, update, sem):
+    width = update.shape[1]
     low = GROUP // BLOCK * LOW
-
-    def spread_rows(c):
-        return dot(spread[...], jnp.concatenate([c, c], axis=0)).astype(BF16)
-
-    own_rows = spread_rows(own[...])
-    mean_rows = spread_rows(mean[...])
+    n = pl.program_id(0)
+
+    def copy(n):
+        here = pl.ds(pl.multiple_of(n * width, width), width)
+        return pltpu.make_async_copy(fresh_in.at[:, here], fresh.at[0, :, here], sem.at[n])
+
+    copy(n).start()
+    coeff = mean[:, pl.ds(pl.multiple_of(n * (width // BLOCK * LOW), 128), width // BLOCK * LOW)]
+    mean_rows = dot(spread[...], jnp.concatenate([coeff, coeff], axis=0)).astype(BF16)
     for s in range(width // GROUP):
-        here = slice(s * GROUP, (s + 1) * GROUP)
-        lanes = slice(s * low, (s + 1) * low)
-        tok = g[:, :, here].reshape(at.shape[1], GROUP)
-        full = momentum_decay * momentum[0, :, here].astype(jnp.float32) + dot(at[...], tok)
-        piece = own_rows[:, lanes]
-        shaped = dot(jnp.concatenate([piece, piece], axis=1), unfold[...])
-        fresh[0, :, here] = (full - shaped).astype(BF16)
-        piece = mean_rows[:, lanes]
-        update[:, here] = dot(jnp.concatenate([piece, piece], axis=1), unfold[...]).astype(BF16)
+        piece = mean_rows[:, s * low:(s + 1) * low]
+        update[:, s * GROUP:(s + 1) * GROUP] = dot(
+            jnp.concatenate([piece, piece], axis=1), unfold[...]
+        ).astype(BF16)
+
+    @pl.when(n == sem.shape[0] - 1)
+    def _():
+        for k in range(sem.shape[0]):
+            copy(k).wait()
 
 
 def shards(n_rep, n_fsdp, acts, grad_out, momentum, band):
@@ -346,35 +350,34 @@
     vmem = pl.BlockSpec(memory_space=pltpu.VMEM)
     hbm = pl.BlockSpec(memory_space=pl.ANY)
     dma = pltpu.SemaphoreType.DMA
-    at, g, own, mean = pl.pallas_call(
+    fresh_in, mean = pl.pallas_call(
         functools.partial(gather_kernel, n_rep, n_fsdp, width, chunks),
         out_shape=(
-            jax.ShapeDtypeStruct((rows, tokens), BF16),
-            jax.ShapeDtypeStruct((n_fsdp, toks, cols), BF16),
-            jax.ShapeDtypeStruct((low_rows, low_cols), BF16),
-            jax.ShapeDtypeStruct((low_rows, low_cols), BF16),
-        ),
-        in_specs=[pl.BlockSpec(memory_space=pltpu.SMEM), hbm, hbm, hbm, vmem, vmem, vmem],
-        out_specs=(hbm, hbm, vmem, vmem),
+            pltpu.VMEM((rows, cols), BF16),
+            pltpu.VMEM((low_rows, low_cols), BF16),
+        ),
+        in_specs=[pl.BlockSpec(memory_space=pltpu.SMEM), hbm, hbm, hbm] + [vmem] * 5,
+        out_specs=(vmem, vmem),
         scratch_shapes=[
             pltpu.VMEM((n_fsdp, toks, rows), BF16),
             pltpu.VMEM((n_fsdp, toks, cols), BF16),
             pltpu.VMEM((rows, tokens), BF16),
             pltpu.VMEM((2, rows, width), BF16),
+            pltpu.VMEM((rows, width), jnp.float32),
             pltpu.VMEM((n_rep, low_rows, low_cols), BF16),
             pltpu.VMEM((low_rows, low_width), jnp.float32),
             dma((n_fsdp,)), dma((n_fsdp,)), dma, dma,
             dma((n_fsdp, chunks)), dma((places, chunks)), dma((chunks,)), dma((places, chunks)),
-            dma((2,)), dma((n_rep, chunks)), dma((n_rep, chunks)), dma((chunks,)), dma,
+            dma((2,)), dma((n_rep, chunks)), dma((n_rep, chunks)),
         ],
         compiler_params=pltpu.CompilerParams(
-            collective_id=0, has_side_effects=True, vmem_limit_bytes=56 * 2**20
+            collective_id=0, has_side_effects=True, vmem_limit_bytes=44 * 2**20
         ),
         cost_estimate=pl.CostEstimate(
             flops=4 * rows * tokens * cols, bytes_accessed=2 * rows * cols, transcendentals=0
         ),
         name="gather",
-    )(band, acts, grad_out, momentum, fold, rh, rl)
+    )(band, acts, grad_out, momentum, fold, rh, rl, unfold, spread)
     fresh, update = pl.pallas_call(
         finish_kernel,
         grid=(cols // 1024,),
@@ -384,23 +387,21 @@
         ),
         in_specs=[
             vmem,
-            pl.BlockSpec((n_fsdp, toks, 1024), lambda n: (0, 0, n)),
-            pl.BlockSpec((1, rows, 1024), lambda n: (0, 0, n)),
-            pl.BlockSpec((low_rows, 256), lambda n: (0, n)),
-            pl.BlockSpec((low_rows, 256), lambda n: (0, n)),
+            vmem,
             vmem,
             vmem,
         ],
         out_specs=(
-            pl.BlockSpec((1, rows, 1024), lambda n: (0, 0, n)),
+            hbm,
             pl.BlockSpec((rows, 1024), lambda n: (0, n)),
         ),
-        compiler_params=pltpu.CompilerParams(vmem_limit_bytes=56 * 2**20),
+        scratch_shapes=[dma((cols // 1024,))],
+        compiler_params=pltpu.CompilerParams(vmem_limit_bytes=24 * 2**20),
         cost_estimate=pl.CostEstimate(
             flops=8 * rows * tokens * cols, bytes_accessed=7 * rows * cols, transcendentals=0
         ),
         name="finish",
-    )(at, g, momentum, own, mean, unfold, spread)
+    )(fresh_in, mean, unfold, spread)
     return fresh, update
 
 

time: 116 us -> 102 us (0.88)
  Pallas kernels: 115 us -> 101 us
    pallas_call x1, Pallas kernels: 25.2 us -> 12.2 us  [shards(): pl.pallas_call(finish_kernel, grid=(cols // 1024,), out_shape=(jax.ShapeD...]
where the time goes in v2:
time: 102 us
  Pallas kernels  101 us (99%)
    pallas_call x1, Pallas kernels, shards(): pl.pallas_call(functools.partial(gather_kernel, n_rep, n_fsdp, width, chu...  88.7 us
    pallas_call x1, Pallas kernels, shards(): pl.pallas_call(finish_kernel, grid=(cols // 1024,), out_shape=(jax.ShapeD...  12.2 us

profile of v2, /device:TPU:0, one launch (start us, length us, event | category | flops | bytes accessed | tf_op | source)
XLA Modules:
  0.0 101.6 jit_solution(697070270179841864)
XLA Ops:
  0.6 0.0 copy-start
  0.6 0.0 copy-start.1
  0.7 88.7 %gather.1 = (bf16[512,14336]{1,0:T(8,128)(2,1)S(1)}, bf16[128,3584]{1,0:T(8,128)(2,1)S(1)}) custom-call(s32[32]{0:T(128)} %band.1, bf16[32,4096]{1,0:T(8,128)(2,1)} %acts.1, bf16[32,14336]{1,0:T(8,128)(2,1)} %gout.1, bf16[1,512,14336]{2,1,0:T(8,128)(2,1)} %momentum.1, bf16[512,256]{1,0:T(8,128)(2,1)} %constant.8.clone.fold.spread, ...), custom_call_target="tpu_custom_call" | custom-call | flops 7516192768 | bytes 14680064 | tf_op jit(solution)/shard_map/gather/pallas_call | solution.py:353
  89.3 0.0 copy-done
  89.3 0.0 copy-done.1
  89.3 12.2 %finish.1 = (bf16[1,512,14336]{2,1,0:T(8,128)(2,1)}, bf16[512,14336]{1,0:T(8,128)(2,1)}) custom-call(bf16[512,14336]{1,0:T(8,128)(2,1)S(1)} %get-tuple-element.4.fresh_in, bf16[128,3584]{1,0:T(8,128)(2,1)S(1)} %get-tuple-element.5.mean, bf16[256,512]{1,0:T(8,128)(2,1)S(1)} %copy-done, bf16[512,256]{1,0:T(8,128)(2,1)S(1)} %copy-done.1), custom_call_target="tpu_custom_call" | custom-call | flops 15032385536 | bytes 51380224 | tf_op jit(solution)/shard_map/finish/pallas_call | solution.py:381
Async XLA Ops:
  0.6 88.7 %copy-start = (bf16[256,512]{1,0:T(8,128)(2,1)S(1)}, bf16[256,512]{1,0:T(8,128)(2,1)}, u32[]{:S(2)}) copy-start(bf16[256,512]{1,0:T(8,128)(2,1)} %constant.9.clone.unfold) | copy-start | bytes 786436
  0.6 88.7 %copy-start.1 = (bf16[512,256]{1,0:T(8,128)(2,1)S(1)}, bf16[512,256]{1,0:T(8,128)(2,1)}, u32[]{:S(2)}) copy-start(bf16[512,256]{1,0:T(8,128)(2,1)} %constant.8.clone.fold.spread) | copy-start | bytes 786436

commit v3 on v2

--- a/solution.py
+++ b/solution.py
@@ -319,7 +319,11 @@
         here = pl.ds(pl.multiple_of(n * width, width), width)
         return pltpu.make_async_copy(fresh_in.at[:, here], fresh.at[0, :, here], sem.at[n])
 
-    copy(n).start()
+    @pl.when(n == 0)
+    def _():
+        for k in range(sem.shape[0]):
+            copy(k).start()
+
     coeff = mean[:, pl.ds(pl.multiple_of(n * (width // BLOCK * LOW), 128), width // BLOCK * LOW)]
     mean_rows = dot(spread[...], jnp.concatenate([coeff, coeff], axis=0)).astype(BF16)
     for s in range(width // GROUP):

time: 102 us -> 105 us (1.029)
  Pallas kernels: 101 us -> 104 us
    pallas_call x1, Pallas kernels: 12.2 us -> 15.6 us  [shards(): pl.pallas_call(finish_kernel, grid=(cols // 1024,), out_shape=(jax.ShapeD...]
where the time goes in v3:
time: 105 us
  Pallas kernels  104 us (99%)
    pallas_call x1, Pallas kernels, shards(): pl.pallas_call(functools.partial(gather_kernel, n_rep, n_fsdp, width, chu...  88.7 us
    pallas_call x1, Pallas kernels, shards(): pl.pallas_call(finish_kernel, grid=(cols // 1024,), out_shape=(jax.ShapeD...  15.6 us

profile of v3, /device:TPU:0, one launch (start us, length us, event | category | flops | bytes accessed | tf_op | source)
XLA Modules:
  0.0 104.9 jit_solution(16941394298356752672)
XLA Ops:
  0.6 0.0 copy-start
  0.6 0.0 copy-start.1
  0.7 88.7 %gather.1 = (bf16[512,14336]{1,0:T(8,128)(2,1)S(1)}, bf16[128,3584]{1,0:T(8,128)(2,1)S(1)}) custom-call(s32[32]{0:T(128)} %band.1, bf16[32,4096]{1,0:T(8,128)(2,1)} %acts.1, bf16[32,14336]{1,0:T(8,128)(2,1)} %gout.1, bf16[1,512,14336]{2,1,0:T(8,128)(2,1)} %momentum.1, bf16[512,256]{1,0:T(8,128)(2,1)} %constant.8.clone.fold.spread, ...), custom_call_target="tpu_custom_call" | custom-call | flops 7516192768 | bytes 14680064 | tf_op jit(solution)/shard_map/gather/pallas_call | solution.py:357
  89.3 0.0 copy-done
  89.3 0.0 copy-done.1
  89.3 15.6 %finish.1 = (bf16[1,512,14336]{2,1,0:T(8,128)(2,1)}, bf16[512,14336]{1,0:T(8,128)(2,1)}) custom-call(bf16[512,14336]{1,0:T(8,128)(2,1)S(1)} %get-tuple-element.4.fresh_in, bf16[128,3584]{1,0:T(8,128)(2,1)S(1)} %get-tuple-element.5.mean, bf16[256,512]{1,0:T(8,128)(2,1)S(1)} %copy-done, bf16[512,256]{1,0:T(8,128)(2,1)S(1)} %copy-done.1), custom_call_target="tpu_custom_call" | custom-call | flops 15032385536 | bytes 51380224 | tf_op jit(solution)/shard_map/finish/pallas_call | solution.py:385
Async XLA Ops:
  0.6 88.7 %copy-start = (bf16[256,512]{1,0:T(8,128)(2,1)S(1)}, bf16[256,512]{1,0:T(8,128)(2,1)}, u32[]{:S(2)}) copy-start(bf16[256,512]{1,0:T(8,128)(2,1)} %constant.9.clone.unfold) | copy-start | bytes 786436
  0.6 88.7 %copy-start.1 = (bf16[512,256]{1,0:T(8,128)(2,1)S(1)}, bf16[512,256]{1,0:T(8,128)(2,1)}, u32[]{:S(2)}) copy-start(bf16[512,256]{1,0:T(8,128)(2,1)} %constant.8.clone.fold.spread) | copy-start | bytes 786436
